TPU v7x, 32 devices: a whole 2x2x4 slice. The times are simulated.
32 devices in a mesh: groups: 2 (over x), pool: 8 (over z, y), tensor: 2 (over core).
Axes of the slice: x: 2, y: 2, z: 4, core: 2. Of those that a mesh axis runs over, the one named last changes fastest.
Arguments:
- queries: bfloat16 [4096, 32, 128], P(('groups', 'pool'), 'tensor'), parts along dimension 0, may hold values from -8 to 8, as said below
- turn_cache: bfloat16 [4096, 2, 4, 128], P(('groups', 'pool'), None, 'tensor'), parts along dimension 0, may hold values from -6 to 6, as said below
- page_pool: bfloat16 [2560, 32, 2, 4, 128], P(('groups', 'pool'), None, None, 'tensor'), parts along dimension 0, may hold values from -6 to 6
- prefix_tokens: int32 [16], P('groups'), parts along dimension 0, may hold values from 2048 to 4096, as said below
- prefix_table: int32 [16, 128], P('groups'), parts along dimension 0, may hold values from 0 to 1279, as said below
- write_table: int32 [16, 8], P('groups'), parts along dimension 0, may hold values from 0 to 1279, as said below
- assignment: int32 [16], P('groups'), parts along dimension 0, may hold values from 0 to 7, each once
Outputs:
- attention: bfloat16 [4096, 32, 128], P(('groups', 'pool'), 'tensor'), parts along dimension 0
- updated_pool: bfloat16 [2560, 32, 2, 4, 128], P(('groups', 'pool'), None, None, 'tensor'), parts along dimension 0
There are 2 independent parts, one for each index of `groups`. A program takes and returns all parts, laid end to end along the dimension named above; each array names one. Nothing has to cross between parts.
Inputs may be any that keep to these rules, and one draw needn't show every extreme that they name: `queries`: A float draw. `turn_cache`: A float draw. `prefix_tokens`: some conversation's prefix has exactly 4096 tokens. `prefix_table`: entry [c, j] is owner * 160 + slot, the page that holds prefix tokens j * 32 to (j + 1) * 32 - 1 of conversation c; entries past the prefix's last page are unused. Among one conversation's used pages at most 17 lie on one owner, and for every conversation exactly 17 lie on some owner. Slots are below 152. `write_table`: entry [c, j] is owner * 160 + slot; the pages of one conversation lie on different owners, all entries are distinct, and slots are 152 or more. `assignment`: each conversation is prefilled by one pool index.
All inputs are finite; a program needn't handle non-finite values.
Results may differ from a plain program's by a relative error of at most 0.004.
Values may be sent and summed in bfloat16 or wider, within the bound.
A program may use at most 128 MiB of HBM per device.

v0:
```python
import functools

import jax
import jax.numpy as jnp
from jax import lax
from jax.experimental import pallas as pl
from jax.experimental.pallas import tpu as pltpu
from jax.sharding import PartitionSpec as P

LOG2E = 1.4426950408889634
HIDDEN = -1e30


def partner_pair(me, step, n):
    if n & (n - 1) == 0:
        other = 0
        bit = 1
        while bit < n:
            other = other + ((me // bit + step // bit) % 2) * bit
            bit *= 2
        return other, other
    return (me + step) % n, (me + n - step) % n


def kernel(
    n, cap, page_rows, row_block, slots_ref, seen_ref, fresh_pick_ref, q_ref, turn_ref, pool_ref,
    out_ref, written_ref,
    stage, recv, fresh_stage, fresh_recv, q_scr, wide, split, bias, m_scr, l_scr, acc,
    send_sem, recv_sem, fresh_send_sem, fresh_recv_sem,
):
    me = lax.axis_index("pool")
    new_len = q_ref.shape[0]
    head_dim = q_ref.shape[2]
    total_rows = q_scr.shape[1]
    page = page_rows // 4
    block_tokens = cap * page
    factor = head_dim ** (-0.5) * LOG2E

    barrier = pltpu.get_barrier_semaphore()

    @pl.loop(1, n)
    def _(step):
        to, source = partner_pair(me, step, n)
        pl.semaphore_signal(barrier, inc=1, device_id={"pool": to}, device_id_type=pl.DeviceIdType.MESH)

    def block_copy(step):
        to, source = partner_pair(me, step, n)
        return pltpu.make_async_remote_copy(
            src_ref=stage.at[step], dst_ref=recv.at[step],
            send_sem=send_sem.at[step], recv_sem=recv_sem.at[step],
            device_id={"pool": to}, device_id_type=pl.DeviceIdType.MESH,
        )

    def fresh_copy(step):
        to, source = partner_pair(me, step, n)
        return pltpu.make_async_remote_copy(
            src_ref=fresh_stage.at[step], dst_ref=fresh_recv.at[step],
            send_sem=fresh_send_sem.at[step], recv_sem=fresh_recv_sem.at[step],
            device_id={"pool": to}, device_id_type=pl.DeviceIdType.MESH,
        )

    def fill(step):
        to, source = partner_pair(me, step, n)
        for rank in range(cap):
            stage[step, pl.ds(rank * page_rows, page_rows), :] = pool_ref[slots_ref[to, rank]]

    fill(n - 1)
    pl.semaphore_wait(barrier, n - 1)
    block_copy(n - 1).start()

    @pl.loop(1, n - 1)
    def _(index):
        step = n - 1 - index
        fill(step)
        block_copy(step).start()

    @pl.loop(1, n)
    def _(step):
        to, source = partner_pair(me, step, n)
        fresh_stage[step] = turn_ref[fresh_pick_ref[to]]
        fresh_copy(step).start()

    written_ref[me] = turn_ref[fresh_pick_ref[me]]
    fill(0)

    for h in range(2):
        picked = q_ref[...].astype(jnp.float32)[:, h * 8:(h + 1) * 8, :]
        q_scr[h] = picked.reshape(total_rows, head_dim).astype(jnp.bfloat16)

    def separate(rows, tokens):
        wide[0:tokens * 4, :] = rows.astype(jnp.float32)
        for part in range(4):
            split[part, 0:tokens, :] = wide[pl.ds(part, tokens, stride=4), :].astype(jnp.bfloat16)

    def scores_of(h, start, tokens):
        return lax.dot_general(
            split[h, 0:tokens, :], q_scr[h, pl.ds(start, row_block), :],
            (((1,), (1,)), ((), ())), preferred_element_type=jnp.float32,
        )

    def weigh(h, weights, tokens):
        return lax.dot_general(
            split[2 + h, 0:tokens, :], weights.astype(jnp.bfloat16),
            (((0,), (0,)), ((), ())), preferred_element_type=jnp.float32,
        )

    separate(turn_ref[...].reshape(new_len * 4, head_dim), new_len)

    @pl.loop(0, total_rows // row_block)
    def _(index):
        start = pl.multiple_of(index * row_block, row_block)
        key = lax.broadcasted_iota(jnp.int32, (new_len, row_block), 0)
        query = lax.broadcasted_iota(jnp.int32, (new_len, row_block), 1) + start
        for h in range(2):
            s = jnp.where(key * 8 <= query, scores_of(h, start, new_len), HIDDEN)
            top = jnp.max(s, axis=0, keepdims=True)
            weights = jnp.exp2((s - top) * factor)
            m_scr[h, :, pl.ds(start, row_block)] = top
            l_scr[h, :, pl.ds(start, row_block)] = jnp.sum(weights, axis=0, keepdims=True)
            acc[h, :, pl.ds(start, row_block)] = weigh(h, weights, new_len)

    def attend(block_ref, source):
        token = lax.broadcasted_iota(jnp.int32, (page, 128), 0)
        for rank in range(cap):
            bias[pl.ds(rank * page, page), :] = jnp.where(token < seen_ref[source, rank], 0.0, HIDDEN)
        separate(block_ref[...], block_tokens)

        @pl.loop(0, total_rows // row_block)
        def _(index):
            start = pl.multiple_of(index * row_block, row_block)
            columns = pl.ds(start, row_block)
            hide = jnp.concatenate([bias[...]] * (row_block // 128), axis=1)
            for h in range(2):
                s = scores_of(h, start, block_tokens) + hide
                before = m_scr[h, :, columns]
                top = jnp.maximum(before, jnp.max(s, axis=0, keepdims=True))
                shrink = jnp.exp2((before - top) * factor)
                weights = jnp.exp2((s - top) * factor)
                m_scr[h, :, columns] = top
                l_scr[h, :, columns] = l_scr[h, :, columns] * shrink + jnp.sum(weights, axis=0, keepdims=True)
                acc[h, :, columns] = acc[h, :, columns] * shrink + weigh(h, weights, block_tokens)

    attend(stage.at[0], me)

    @pl.loop(1, n)
    def _(step):
        to, source = partner_pair(me, step, n)
        block_copy(step).wait_recv()
        attend(recv.at[step], source)

    @pl.loop(1, n)
    def _(step):
        to, source = partner_pair(me, step, n)
        fresh_copy(step).wait_recv()
        written_ref[source] = fresh_recv[step]

    out_block = row_block // 8

    @pl.loop(0, total_rows // row_block)
    def _(index):
        start = pl.multiple_of(index * row_block, row_block)
        columns = pl.ds(start, row_block)
        halves = []
        for h in range(2):
            mixed = acc[h, :, columns] / l_scr[h, :, columns]
            halves.append(mixed.T.reshape(out_block, 8, head_dim))
        out_ref[pl.ds(index * out_block, out_block)] = jnp.concatenate(halves, axis=1).astype(jnp.bfloat16)

    @pl.loop(1, n)
    def _(step):
        block_copy(step).wait_send()
        fresh_copy(step).wait_send()


def shards(queries, turn_cache, page_pool, prefix_tokens, prefix_table, write_table, assignment):
    n = lax.axis_size("pool")
    device = lax.axis_index("pool")
    pool_dev, page_size = page_pool.shape[0], page_pool.shape[1]
    head_dim = page_pool.shape[4]
    new_len = queries.shape[0]
    max_pages = prefix_table.shape[1]
    cap = (max_pages + n - 1) // n + 1
    page_rows = page_size * 4
    page_index = jnp.arange(max_pages)
    peer_index = jnp.arange(n)

    ordered = prefix_table[assignment]
    lengths = prefix_tokens[assignment]
    own_row = ordered[device]
    own_length = lengths[device]
    used = page_index[None, :] * page_size < lengths[:, None]
    requested = (ordered // pool_dev == device) & used
    from_peer = (own_row[None, :] // pool_dev == peer_index[:, None]) & (page_index[None, :] * page_size < own_length)
    marked = jnp.concatenate([requested, from_peer], axis=0)
    seen_count = jnp.minimum(own_length - page_index * page_size, page_size)
    values = jnp.concatenate([ordered % pool_dev, jnp.broadcast_to(seen_count[None, :], (n, max_pages))], axis=0)
    earlier = page_index[:, None] < page_index[None, :]
    rank = jnp.sum((marked[:, :, None] & earlier[None]).astype(jnp.int32), axis=1)
    pick = marked[:, None, :] & (rank[:, None, :] == jnp.arange(cap)[None, :, None])
    picked = jnp.sum(jnp.where(pick, values[:, None, :], 0), axis=2)
    slots, seen = picked[:n], picked[n:]

    incoming_write = write_table[assignment]
    own_write = incoming_write[device]
    write_hit = (own_write // pool_dev)[None, :] == peer_index[:, None]
    fresh_pick = jnp.sum(jnp.where(write_hit, jnp.arange(own_write.shape[0])[None, :], 0), axis=1)
    write_in = incoming_write // pool_dev == device
    target_slot = jnp.where(
        jnp.any(write_in, axis=1),
        jnp.sum(jnp.where(write_in, incoming_write % pool_dev, 0), axis=1),
        pool_dev,
    )

    total_rows = new_len * 8
    row_block = 512
    tokens = cap * page_size
    smem = pl.BlockSpec(memory_space=pltpu.SMEM)
    vmem = pl.BlockSpec(memory_space=pltpu.VMEM)
    bf16, f32 = jnp.bfloat16, jnp.float32
    attention, written = pl.pallas_call(
        functools.partial(kernel, n, cap, page_rows, row_block),
        out_shape=(
            jax.ShapeDtypeStruct(queries.shape, bf16),
            jax.ShapeDtypeStruct((n, page_rows, head_dim), bf16),
        ),
        in_specs=[smem, smem, smem, vmem, vmem, vmem],
        out_specs=(vmem, vmem),
        scratch_shapes=[
            pltpu.VMEM((n, cap * page_rows, head_dim), bf16),
            pltpu.VMEM((n, cap * page_rows, head_dim), bf16),
            pltpu.VMEM((n, page_rows, head_dim), bf16),
            pltpu.VMEM((n, page_rows, head_dim), bf16),
            pltpu.VMEM((2, total_rows, head_dim), bf16),
            pltpu.VMEM((max(tokens, new_len) * 4, head_dim), f32),
            pltpu.VMEM((4, max(tokens, new_len), head_dim), bf16),
            pltpu.VMEM((tokens, 128), f32),
            pltpu.VMEM((2, 1, total_rows), f32),
            pltpu.VMEM((2, 1, total_rows), f32),
            pltpu.VMEM((2, head_dim, total_rows), f32),
            pltpu.SemaphoreType.DMA((n,)),
            pltpu.SemaphoreType.DMA((n,)),
            pltpu.SemaphoreType.DMA((n,)),
            pltpu.SemaphoreType.DMA((n,)),
        ],
        compiler_params=pltpu.CompilerParams(
            collective_id=0, has_side_effects=True, vmem_limit_bytes=48 * 1024 * 1024
        ),
    )(
        slots, seen, fresh_pick, queries,
        turn_cache.reshape(new_len // page_size, page_rows, head_dim),
        page_pool.reshape(pool_dev, page_rows, head_dim),
    )
    updated_pool = page_pool.at[target_slot].set(
        written.reshape((n,) + page_pool.shape[1:]), mode="drop"
    )
    return (attention, updated_pool)


def solution(mesh):
    placed = (
        P(("groups", "pool"), "tensor", None),
        P(("groups", "pool"), None, "tensor", None),
        P(("groups", "pool"), None, None, "tensor", None),
        P("groups"),
        P("groups", None),
        P("groups", None),
        P("groups"),
    )
    return jax.shard_map(
        shards,
        mesh=mesh,
        in_specs=placed,
        out_specs=(
            P(("groups", "pool"), "tensor", None),
            P(("groups", "pool"), None, None, "tensor", None),
        ),
        check_vma=False,
    )
```

profile of v0, /device:TPU:0, one launch (start us, length us, event | category | flops | bytes accessed | tf_op | source)
XLA Modules:
  0.0 163.8 jit_solution(9546962901445240833)
XLA Ops:
  0.6 0.0 copy-start
  0.6 0.0 copy-start.1
  0.7 0.0 copy-start.2
  0.7 0.0 copy-start.3
  0.7 0.0 copy-start.4
  0.7 0.0 copy-start.5
  0.7 14.5 %copy.16 = bf16[160,32,2,2,128]{4,3,2,1,0:T(2,128)(2,1)} copy(bf16[160,32,2,2,128]{4,3,2,1,0:T(2,128)(2,1)} %param.9) | data formatting | bytes 10485760
  15.2 0.0 copy-done.5
  15.2 0.0 copy-done.3
  15.3 0.6 gather_fusion.1
  15.9 0.6 dynamic_slice.10
  16.5 0.6 subtract_minimum_fusion
  17.1 0.7 broadcast_compare_fusion
  17.8 0.0 copy-done
  17.8 0.6 gather_fusion
  18.4 0.0 copy-done.4
  18.4 0.6 gather_fusion.2
  19.0 0.1 fusion.4
  19.1 0.1 fusion.6
  19.2 0.1 select_reduce_fusion.1.fresh_pick_ref
  19.4 0.1 reduce_or.9
  19.5 0.3 convert_reduce_fusion
  19.9 0.4 select_reduce_fusion
  20.2 0.1 fusion.12
  20.3 0.1 copy.12.seen_ref
  20.4 0.1 copy.11.slots_ref
  20.5 0.0 copy-done.1
  20.5 0.0 copy-done.2
  20.5 140.0 %shard_map.86 = (bf16[256,16,128]{2,1,0:T(8,128)(2,1)S(1)}, bf16[8,128,128]{2,1,0:T(8,128)(2,1)S(1)}) custom-call(s32[8,17]{1,0:T(8,128)S(1)} %copy.11.slots_ref, s32[8,17]{1,0:T(8,128)S(1)} %copy.12.seen_ref, s32[8]{0:T(128)S(1)} %select_reduce_fusion.1.fresh_pick_ref, bf16[256,16,128]{2,1,0:T(8,128)(2,1)S(1)} %copy-done.1, ...), custom_call_target="tpu_custom_call" | custom-call | tf_op jit(solution)/shard_map/pallas_call | solution.py:220
  160.5 2.3 %scatter_fusion = bf16[160,32,2,2,128]{4,3,2,1,0:T(2,128)(2,1)} fusion(bf16[160,32,2,2,128]{4,3,2,1,0:T(2,128)(2,1)} %copy.16, s32[8]{0:T(128)S(1)} %fusion.8, bf16[8,32,2,2,128]{4,3,2,1,0:T(2,128)(2,1)S(1)} %bitcast.13), kind=kCustom, calls=%fused_computation.3 | custom fusion | bytes 786464 | tf_op jit(solution)/shard_map/scatter | solution.py:253
  162.8 1.0 copy.17
  (11 shorter events, 0.1 us)
Async XLA Ops:
  0.6 17.2 %copy-start = (s32[8,128]{1,0:T(8,128)S(1)}, s32[8,128]{1,0:T(8,128)}, u32[]{:S(2)}) copy-start(s32[8,128]{1,0:T(8,128)} %param.11) | copy-start | bytes 12292
  0.6 19.8 %copy-start.1 = (bf16[256,16,128]{2,1,0:T(8,128)(2,1)S(1)}, bf16[256,16,128]{2,1,0:T(8,128)(2,1)}, u32[]{:S(2)}) copy-start(bf16[256,16,128]{2,1,0:T(8,128)(2,1)} %q_ref.1) | copy-start | bytes 3145732
  0.7 19.8 %copy-start.2 = (bf16[256,2,2,128]{3,2,1,0:T(2,128)(2,1)S(1)}, bf16[256,2,2,128]{3,2,1,0:T(2,128)(2,1)}, u32[]{:S(2)}) copy-start(bf16[256,2,2,128]{3,2,1,0:T(2,128)(2,1)} %param.8) | copy-start | bytes 786436
  0.7 14.6 %copy-start.3 = (s32[8]{0:T(128)S(1)}, s32[8]{0:T(128)}, u32[]{:S(2)}) copy-start(s32[8]{0:T(128)} %param.10) | copy-start | bytes 100
  0.7 17.7 %copy-start.4 = (s32[8,8]{1,0:T(8,128)S(1)}, s32[8,8]{1,0:T(8,128)}, u32[]{:S(2)}) copy-start(s32[8,8]{1,0:T(8,128)} %param.12) | copy-start | bytes 772
  0.7 14.5 %copy-start.5 = (s32[8]{0:T(128)S(1)}, s32[8]{0:T(128)}, u32[]{:S(2)}) copy-start(s32[8]{0:T(128)} %param.13) | copy-start | bytes 100
where the time goes:
time: 164 us
  Pallas kernels  140 us (85%)
  local copies, waits for them, and re-layouts  20.4 us (12%)
  other arithmetic  2.56 us (2%)
    pallas_call x1, Pallas kernels, shards(): pl.pallas_call(functools.partial(kernel, n, cap, page_rows, row_block), o...  140 us
    unnamed x16, local copies, waits for them, and re-layouts  15.7 us

commit v1 on v0

v1 whole, which is shorter than its diff:
```python
import functools

import jax
import jax.numpy as jnp
from jax import lax
from jax.experimental import pallas as pl
from jax.experimental.pallas import tpu as pltpu
from jax.sharding import PartitionSpec as P

LOG2E = 1.4426950408889634
HIDDEN = -1e30


def partner_pair(me, step, n):
    if n & (n - 1) == 0:
        other = 0
        bit = 1
        while bit < n:
            other = other + ((me // bit + step // bit) % 2) * bit
            bit *= 2
        return other, other
    return (me + step) % n, (me + n - step) % n


def kernel(
    n, cap, wave, page_rows, row_block, plan_ref, q_hbm, turn_hbm, pool_hbm,
    out_ref, written_ref,
    q_ref, turn_ref, pool_ref, load_sem,
    stage, recv, rest_recv, fresh_stage, fresh_recv, q_scr, wide, split, bias, m_scr, l_scr, acc,
    send_sem, recv_sem, fresh_send_sem, fresh_recv_sem,
):
    me = lax.axis_index("pool")
    new_len = q_ref.shape[0]
    head_dim = q_ref.shape[2]
    total_rows = q_scr.shape[1]
    page = page_rows // 4
    full, rest = cap // wave, cap % wave
    factor = head_dim ** (-0.5) * LOG2E

    pool_load = pltpu.make_async_copy(pool_hbm, pool_ref, load_sem.at[0])
    turn_load = pltpu.make_async_copy(turn_hbm, turn_ref, load_sem.at[1])
    q_load = pltpu.make_async_copy(q_hbm, q_ref, load_sem.at[2])
    pool_load.start()
    turn_load.start()
    q_load.start()

    barrier = pltpu.get_barrier_semaphore()

    @pl.loop(1, n)
    def _(step):
        to, source = partner_pair(me, step, n)
        pl.semaphore_signal(barrier, inc=1, device_id={"pool": to}, device_id_type=pl.DeviceIdType.MESH)

    def remote(src, dst, send, receive, step):
        to, source = partner_pair(me, step, n)
        return pltpu.make_async_remote_copy(
            src_ref=src, dst_ref=dst, send_sem=send, recv_sem=receive,
            device_id={"pool": to}, device_id_type=pl.DeviceIdType.MESH,
        )

    def wave_copy(w, step):
        rows = pl.ds(pl.multiple_of(w * (wave * page_rows), page_rows), wave * page_rows)
        return remote(stage.at[step, rows], recv.at[w, step - 1], send_sem.at[w, step], recv_sem.at[w, step], step)

    def rest_copy(step):
        rows = pl.ds(full * wave * page_rows, rest * page_rows)
        return remote(stage.at[step, rows], rest_recv.at[step - 1], send_sem.at[full, step], recv_sem.at[full, step], step)

    def fresh_copy(step):
        return remote(fresh_stage.at[step], fresh_recv.at[step], fresh_send_sem.at[step], fresh_recv_sem.at[step], step)

    def fill(step, first, count):
        to, source = partner_pair(me, step, n)
        for r in range(count):
            rows = pl.ds(pl.multiple_of((first + r) * page_rows, page_rows), page_rows)
            stage[step, rows, :] = pool_ref[plan_ref[to, first + r]]

    pool_load.wait()

    @pl.loop(1, n)
    def _(step):
        fill(step, 0, wave)

    pl.semaphore_wait(barrier, n - 1)

    @pl.loop(1, n)
    def _(index):
        wave_copy(0, n - index).start()

    turn_load.wait()

    @pl.loop(1, n)
    def _(step):
        to, source = partner_pair(me, step, n)
        fresh_stage[step] = turn_ref[plan_ref[to, cap]]
        fresh_copy(step).start()

    @pl.loop(1, full)
    def _(w):
        @pl.loop(1, n)
        def _(index):
            fill(n - index, w * wave, wave)
            wave_copy(w, n - index).start()

    if rest:
        @pl.loop(1, n)
        def _(index):
            fill(n - index, full * wave, rest)
            rest_copy(n - index).start()

    written_ref[me] = turn_ref[plan_ref[me, cap]]
    fill(0, 0, cap)

    q_load.wait()
    for h in range(2):
        picked = q_ref[...].astype(jnp.float32)[:, h * 8:(h + 1) * 8, :]
        q_scr[h] = picked.reshape(total_rows, head_dim).astype(jnp.bfloat16)

    def separate(rows, tokens):
        wide[0:tokens * 4, :] = rows.reshape(tokens * 4, head_dim).astype(jnp.float32)
        for part in range(4):
            split[part, 0:tokens, :] = wide[pl.ds(part, tokens, stride=4), :].astype(jnp.bfloat16)

    def scores_of(h, start, tokens):
        return lax.dot_general(
            split[h, 0:tokens, :], q_scr[h, pl.ds(start, row_block), :],
            (((1,), (1,)), ((), ())), preferred_element_type=jnp.float32,
        )

    def weigh(h, weights, tokens):
        return lax.dot_general(
            split[2 + h, 0:tokens, :], weights.astype(jnp.bfloat16),
            (((0,), (0,)), ((), ())), preferred_element_type=jnp.float32,
        )

    separate(turn_ref[...], new_len)

    @pl.loop(0, total_rows // row_block)
    def _(index):
        start = pl.multiple_of(index * row_block, row_block)
        key = lax.broadcasted_iota(jnp.int32, (new_len, row_block), 0)
        query = lax.broadcasted_iota(jnp.int32, (new_len, row_block), 1) + start
        for h in range(2):
            s = jnp.where(key * 8 <= query, scores_of(h, start, new_len), HIDDEN)
            top = jnp.max(s, axis=0, keepdims=True)
            weights = jnp.exp2((s - top) * factor)
            m_scr[h, :, pl.ds(start, row_block)] = top
            l_scr[h, :, pl.ds(start, row_block)] = jnp.sum(weights, axis=0, keepdims=True)
            acc[h, :, pl.ds(start, row_block)] = weigh(h, weights, new_len)

    token = lax.broadcasted_iota(jnp.int32, (page, 128), 0)

    def hide(place, source, rank):
        at = place * page
        rows = pl.ds(at if isinstance(at, int) else pl.multiple_of(at, page), page)
        bias[rows, :] = jnp.where(token < plan_ref[n + source, rank], 0.0, HIDDEN)

    def hide_wave(first, count):
        @pl.loop(1, n)
        def _(step):
            to, source = partner_pair(me, step, n)
            for r in range(count):
                hide((step - 1) * count + r, source, first + r)

    def attend(rows, tokens):
        separate(rows, tokens)

        @pl.loop(0, total_rows // row_block)
        def _(index):
            start = pl.multiple_of(index * row_block, row_block)
            columns = pl.ds(start, row_block)
            hidden = jnp.concatenate([bias[0:tokens, :]] * (row_block // 128), axis=1)
            for h in range(2):
                s = scores_of(h, start, tokens) + hidden
                before = m_scr[h, :, columns]
                top = jnp.maximum(before, jnp.max(s, axis=0, keepdims=True))
                shrink = jnp.exp2((before - top) * factor)
                weights = jnp.exp2((s - top) * factor)
                m_scr[h, :, columns] = top
                l_scr[h, :, columns] = l_scr[h, :, columns] * shrink + jnp.sum(weights, axis=0, keepdims=True)
                acc[h, :, columns] = acc[h, :, columns] * shrink + weigh(h, weights, tokens)

    for rank in range(cap):
        hide(rank, me, rank)
    attend(stage[0], cap * page)

    @pl.loop(0, full)
    def _(w):
        hide_wave(w * wave, wave)

        @pl.loop(1, n)
        def _(step):
            wave_copy(w, step).wait_recv()

        attend(recv[w], (n - 1) * wave * page)

    @pl.loop(1, n)
    def _(step):
        to, source = partner_pair(me, step, n)
        fresh_copy(step).wait_recv()
        written_ref[source] = fresh_recv[step]

    if rest:
        hide_wave(full * wave, rest)

        @pl.loop(1, n)
        def _(step):
            rest_copy(step).wait_recv()

        attend(rest_recv[...], (n - 1) * rest * page)

    out_block = row_block // 8

    @pl.loop(0, total_rows // row_block)
    def _(index):
        start = pl.multiple_of(index * row_block, row_block)
        columns = pl.ds(start, row_block)
        halves = []
        for h in range(2):
            mixed = acc[h, :, columns] / l_scr[h, :, columns]
            halves.append(mixed.T.reshape(out_block, 8, head_dim))
        out_ref[pl.ds(index * out_block, out_block)] = jnp.concatenate(halves, axis=1).astype(jnp.bfloat16)

    @pl.loop(1, n)
    def _(step):
        @pl.loop(0, full)
        def _(w):
            wave_copy(w, step).wait_send()

        if rest:
            rest_copy(step).wait_send()
        fresh_copy(step).wait_send()


def plan_kernel(
    n, cap, pool_dev, page_size, assign_ref, tokens_ref, table_ref, write_ref,
    plan_ref, ordered, lengths, writes,
):
    me = lax.axis_index("pool")
    max_pages = table_ref.shape[1]
    for d in range(n):
        conversation = assign_ref[d]
        ordered[d:d + 1, :] = table_ref[pl.ds(conversation, 1), :]
        lengths[d:d + 1, :] = jnp.full((1, max_pages), tokens_ref[conversation], jnp.int32)
        writes[d:d + 1, :] = write_ref[pl.ds(conversation, 1), :]
    first = lax.broadcasted_iota(jnp.int32, (n, max_pages), 1) * page_size
    slot = ordered[...] - me * pool_dev
    requested = (slot >= 0) & (slot < pool_dev) & (first < lengths[...])
    row = jnp.broadcast_to(ordered[pl.ds(me, 1), :], (n, max_pages))
    length = jnp.broadcast_to(lengths[pl.ds(me, 1), :], (n, max_pages))
    place = row - lax.broadcasted_iota(jnp.int32, (n, max_pages), 0) * pool_dev
    landed = (place >= 0) & (place < pool_dev) & (first < length)
    values = jnp.concatenate([slot, jnp.minimum(length - first, page_size)], axis=0).astype(jnp.float32)
    marked = jnp.concatenate([jnp.where(requested, 1.0, 0.0), jnp.where(landed, 1.0, 0.0)], axis=0)
    earlier = (
        lax.broadcasted_iota(jnp.int32, (max_pages, max_pages), 0)
        < lax.broadcasted_iota(jnp.int32, (max_pages, max_pages), 1)
    )
    rank = jnp.dot(
        marked.astype(jnp.bfloat16), jnp.where(earlier, 1.0, 0.0).astype(jnp.bfloat16),
        preferred_element_type=jnp.float32,
    )
    rank = jnp.where(marked > 0.0, rank, -1.0)
    lane = lax.broadcasted_iota(jnp.int32, (2 * n, max_pages), 1)
    plan = jnp.zeros((2 * n, max_pages), jnp.float32)
    for r in range(cap):
        column = jnp.sum(jnp.where(rank == r, values, 0.0), axis=1, keepdims=True)
        plan = jnp.where(lane == r, column, plan)
    plan_ref[...] = plan.astype(jnp.int32)
    shape = writes.shape
    own = jnp.broadcast_to(writes[pl.ds(me, 1), :], shape)
    there = own - lax.broadcasted_iota(jnp.int32, shape, 0) * pool_dev
    page = lax.broadcasted_iota(jnp.int32, shape, 1).astype(jnp.float32)
    pick = jnp.sum(jnp.where((there >= 0) & (there < pool_dev), page, 0.0), axis=1, keepdims=True)
    here = writes[...] - me * pool_dev
    target = jnp.min(
        jnp.where((here >= 0) & (here < pool_dev), here, pool_dev).astype(jnp.float32), axis=1, keepdims=True
    )
    lane = lane[0:n, :]
    top = plan[0:n, :]
    top = jnp.where(lane == cap, pick, jnp.where(lane == cap + 1, target, top))
    plan_ref[0:n, :] = top.astype(jnp.int32)


def merge_kernel(
    n, cap, pool_dev, plan_ref, written_ref, attention_ref, pool_ref, out_ref, pool_out_ref,
    held, result, in_sem, out_sem, result_sem,
):
    chunks = in_sem.shape[0] - 1
    kept = pool_dev - n
    edges = [kept * chunk // chunks for chunk in range(chunks + 1)] + [pool_dev]
    spans = [pl.ds(low, high - low) for low, high in zip(edges[:-1], edges[1:])]
    loads = [pltpu.make_async_copy(pool_ref.at[span], held.at[span], in_sem.at[c]) for c, span in enumerate(spans)]
    stores = [pltpu.make_async_copy(held.at[span], pool_out_ref.at[span], out_sem.at[c]) for c, span in enumerate(spans)]
    result_in = pltpu.make_async_copy(attention_ref, result, result_sem.at[0])
    result_out = pltpu.make_async_copy(result, out_ref, result_sem.at[1])
    loads[-1].start()
    result_in.start()
    for load in loads[:-1]:
        load.start()
    loads[-1].wait()
    for d in range(n):
        @pl.when(plan_ref[d, cap + 1] < pool_dev)
        def _(d=d):
            held[plan_ref[d, cap + 1]] = written_ref[d]
    stores[-1].start()
    result_in.wait()
    result_out.start()
    for load, store in zip(loads[:-1], stores[:-1]):
        load.wait()
        store.start()
    for store in stores:
        store.wait()
    result_out.wait()


def shards(queries, turn_cache, page_pool, prefix_tokens, prefix_table, write_table, assignment):
    n = lax.axis_size("pool")
    pool_dev, page_size = page_pool.shape[0], page_pool.shape[1]
    head_dim = page_pool.shape[4]
    new_len = queries.shape[0]
    max_pages = prefix_table.shape[1]
    cap = (max_pages + n - 1) // n + 1
    page_rows = page_size * 4
    pages = page_pool.reshape(pool_dev, page_rows, head_dim)
    total_rows = new_len * 8
    row_block = 512
    wave = max(1, 24 // n)
    tokens = max(cap, (n - 1) * wave) * page_size
    smem = pl.BlockSpec(memory_space=pltpu.SMEM)
    vmem = pl.BlockSpec(memory_space=pltpu.VMEM)
    hbm = pl.BlockSpec(memory_space=pl.ANY)
    bf16, f32 = jnp.bfloat16, jnp.float32
    plan = pl.pallas_call(
        functools.partial(plan_kernel, n, cap, pool_dev, page_size),
        out_shape=jax.ShapeDtypeStruct((2 * n, max_pages), jnp.int32),
        in_specs=[smem, smem, vmem, vmem],
        out_specs=vmem,
        scratch_shapes=[
            pltpu.VMEM((n, max_pages), jnp.int32),
            pltpu.VMEM((n, max_pages), jnp.int32),
            pltpu.VMEM((n, write_table.shape[1]), jnp.int32),
        ],
    )(assignment, prefix_tokens, prefix_table, write_table)
    attention, written = pl.pallas_call(
        functools.partial(kernel, n, cap, wave, page_rows, row_block),
        out_shape=(
            jax.ShapeDtypeStruct(queries.shape, bf16),
            jax.ShapeDtypeStruct((n, page_rows, head_dim), bf16),
        ),
        in_specs=[smem, hbm, hbm, hbm],
        out_specs=(vmem, vmem),
        scratch_shapes=[
            pltpu.VMEM(queries.shape, bf16),
            pltpu.VMEM((new_len // page_size, page_rows, head_dim), bf16),
            pltpu.VMEM(pages.shape, bf16),
            pltpu.SemaphoreType.DMA((3,)),
            pltpu.VMEM((n, cap * page_rows, head_dim), bf16),
            pltpu.VMEM((cap // wave, n - 1, wave * page_rows, head_dim), bf16),
            pltpu.VMEM((n - 1, max(cap % wave, 1) * page_rows, head_dim), bf16),
            pltpu.VMEM((n, page_rows, head_dim), bf16),
            pltpu.VMEM((n, page_rows, head_dim), bf16),
            pltpu.VMEM((2, total_rows, head_dim), bf16),
            pltpu.VMEM((max(tokens, new_len) * 4, head_dim), f32),
            pltpu.VMEM((4, max(tokens, new_len), head_dim), bf16),
            pltpu.VMEM((tokens, 128), f32),
            pltpu.VMEM((2, 1, total_rows), f32),
            pltpu.VMEM((2, 1, total_rows), f32),
            pltpu.VMEM((2, head_dim, total_rows), f32),
            pltpu.SemaphoreType.DMA((cap // wave + 1, n)),
            pltpu.SemaphoreType.DMA((cap // wave + 1, n)),
            pltpu.SemaphoreType.DMA((n,)),
            pltpu.SemaphoreType.DMA((n,)),
        ],
        compiler_params=pltpu.CompilerParams(
            collective_id=0, has_side_effects=True, vmem_limit_bytes=56 * 1024 * 1024
        ),
    )(
        plan, queries,
        turn_cache.reshape(new_len // page_size, page_rows, head_dim),
        pages,
    )
    attention, updated_pool = pl.pallas_call(
        functools.partial(merge_kernel, n, cap, pool_dev),
        out_shape=(
            jax.ShapeDtypeStruct(queries.shape, bf16),
            jax.ShapeDtypeStruct(pages.shape, bf16),
        ),
        in_specs=[smem, vmem, hbm, hbm],
        out_specs=(hbm, hbm),
        scratch_shapes=[
            pltpu.VMEM(pages.shape, bf16),
            pltpu.VMEM(queries.shape, bf16),
            pltpu.SemaphoreType.DMA((9,)),
            pltpu.SemaphoreType.DMA((9,)),
            pltpu.SemaphoreType.DMA((2,)),
        ],
        compiler_params=pltpu.CompilerParams(vmem_limit_bytes=56 * 1024 * 1024),
    )(plan, written, attention, pages)
    updated_pool = updated_pool.reshape(page_pool.shape)
    return (attention, updated_pool)


def solution(mesh):
    placed = (
        P(("groups", "pool"), "tensor", None),
        P(("groups", "pool"), None, "tensor", None),
        P(("groups", "pool"), None, None, "tensor", None),
        P("groups"),
        P("groups", None),
        P("groups", None),
        P("groups"),
    )
    return jax.shard_map(
        shards,
        mesh=mesh,
        in_specs=placed,
        out_specs=(
            P(("groups", "pool"), "tensor", None),
            P(("groups", "pool"), None, None, "tensor", None),
        ),
        check_vma=False,
    )
```

time: 164 us -> 128 us (0.78)
  local copies, waits for them, and re-layouts: 20.4 us -> 0 us
  Pallas kernels: 140 us -> 127 us
  other arithmetic: 2.56 us -> 0 us
    unnamed x16 -> x0, local copies, waits for them, and re-layouts: 15.7 us -> none
    pallas_call x1 -> x3, Pallas kernels: 140 us -> 127 us  [the longest x1 119 us: shards(): pl.pallas_call(functools.partial(kernel, n, cap, wave, page_rows, row_blo...]
    scatter x1 -> x0, local copies, waits for them, and re-layouts: 2.31 us -> none  [shards(): page_pool.at[target_slot]]
    gather x3 -> x0, local copies, waits for them, and re-layouts: 1.75 us -> none  [the longest x1 0.64 us: shards(): lengths = prefix_tokens[assignment]]
where the time goes in v1:
time: 128 us; the launch traced here: 127 us
  Pallas kernels  127 us (99%)
    pallas_call x1, Pallas kernels, shards(): pl.pallas_call(functools.partial(kernel, n, cap, wave, page_rows, row_blo...  119 us
    pallas_call x1, Pallas kernels, shards(): pl.pallas_call(functools.partial(merge_kernel, n, cap, pool_dev), out_sha...  6.45 us

profile of v1, /device:TPU:0, one launch (start us, length us, event | category | flops | bytes accessed | tf_op | source)
XLA Modules:
  0.0 127.4 jit_solution(2034322398992089845)
XLA Ops:
  0.6 1.6 %shard_map.86.plan_ref = s32[16,128]{1,0:T(8,128)} custom-call(s32[8]{0:T(128)} %assign_ref.1, s32[8]{0:T(128)} %tokens_ref.1, s32[8,128]{1,0:T(8,128)} %table_ref.1, s32[8,8]{1,0:T(8,128)} %write_ref.1), custom_call_target="tpu_custom_call" | custom-call | tf_op jit(solution)/shard_map/pallas_call | solution.py:334
  2.2 118.7 %shard_map.87 = (bf16[256,16,128]{2,1,0:T(8,128)(2,1)}, bf16[8,128,128]{2,1,0:T(8,128)(2,1)}) custom-call(s32[16,128]{1,0:T(8,128)} %shard_map.86.plan_ref, bf16[256,16,128]{2,1,0:T(8,128)(2,1)} %q_hbm.1, bf16[8,128,128]{2,1,0:T(8,128)(2,1)} %bitcast.5, bf16[160,128,128]{2,1,0:T(8,128)(2,1)} %bitcast.3), custom_call_target="tpu_custom_call" | custom-call | tf_op jit(solution)/shard_map/pallas_call | solution.py:345
  120.9 6.4 %shard_map.88 = (bf16[256,16,128]{2,1,0:T(8,128)(2,1)}, bf16[160,128,128]{2,1,0:T(8,128)(2,1)}) custom-call(s32[16,128]{1,0:T(8,128)} %shard_map.86.plan_ref, bf16[8,128,128]{2,1,0:T(8,128)(2,1)} %get-tuple-element.6.written_ref, bf16[256,16,128]{2,1,0:T(8,128)(2,1)} %get-tuple-element.7.attention_ref, bf16[160,128,128]{2,1,0:T(8,128)(2,1)} %bitcast.4), custom_call_target="tpu_custom_call" | custom-call | tf_op jit(solution)/shard_map/pallas_call | solution.py:383

commit v2 on v1

--- a/solution.py
+++ b/solution.py
@@ -23,9 +23,9 @@
 
 
 def kernel(
-    n, cap, wave, page_rows, row_block, plan_ref, q_hbm, turn_hbm, pool_hbm,
+    n, cap, wave, page_rows, row_block, plan_ref, q_hbm, turn_hbm, pool_ref,
     out_ref, written_ref,
-    q_ref, turn_ref, pool_ref, load_sem,
+    q_ref, turn_ref, load_sem,
     stage, recv, rest_recv, fresh_stage, fresh_recv, q_scr, wide, split, bias, m_scr, l_scr, acc,
     send_sem, recv_sem, fresh_send_sem, fresh_recv_sem,
 ):
@@ -37,10 +37,8 @@
     full, rest = cap // wave, cap % wave
     factor = head_dim ** (-0.5) * LOG2E
 
-    pool_load = pltpu.make_async_copy(pool_hbm, pool_ref, load_sem.at[0])
-    turn_load = pltpu.make_async_copy(turn_hbm, turn_ref, load_sem.at[1])
-    q_load = pltpu.make_async_copy(q_hbm, q_ref, load_sem.at[2])
-    pool_load.start()
+    turn_load = pltpu.make_async_copy(turn_hbm, turn_ref, load_sem.at[0])
+    q_load = pltpu.make_async_copy(q_hbm, q_ref, load_sem.at[1])
     turn_load.start()
     q_load.start()
 
@@ -74,8 +72,6 @@
         for r in range(count):
             rows = pl.ds(pl.multiple_of((first + r) * page_rows, page_rows), page_rows)
             stage[step, rows, :] = pool_ref[plan_ref[to, first + r]]
-
-    pool_load.wait()
 
     @pl.loop(1, n)
     def _(step):
@@ -284,34 +280,29 @@
 
 def merge_kernel(
     n, cap, pool_dev, plan_ref, written_ref, attention_ref, pool_ref, out_ref, pool_out_ref,
-    held, result, in_sem, out_sem, result_sem,
+    tail, held, fresh, out_sem, in_sem,
 ):
-    chunks = in_sem.shape[0] - 1
     kept = pool_dev - n
-    edges = [kept * chunk // chunks for chunk in range(chunks + 1)] + [pool_dev]
-    spans = [pl.ds(low, high - low) for low, high in zip(edges[:-1], edges[1:])]
-    loads = [pltpu.make_async_copy(pool_ref.at[span], held.at[span], in_sem.at[c]) for c, span in enumerate(spans)]
-    stores = [pltpu.make_async_copy(held.at[span], pool_out_ref.at[span], out_sem.at[c]) for c, span in enumerate(spans)]
-    result_in = pltpu.make_async_copy(attention_ref, result, result_sem.at[0])
-    result_out = pltpu.make_async_copy(result, out_ref, result_sem.at[1])
-    loads[-1].start()
+    old = pltpu.make_async_copy(pool_ref.at[pl.ds(0, kept)], pool_out_ref.at[pl.ds(0, kept)], out_sem.at[0])
+    result_in = pltpu.make_async_copy(attention_ref, held, in_sem.at[0])
+    fresh_in = pltpu.make_async_copy(written_ref, fresh, in_sem.at[1])
+    result = pltpu.make_async_copy(held, out_ref, out_sem.at[1])
+    last = pltpu.make_async_copy(tail, pool_out_ref.at[pl.ds(kept, n)], out_sem.at[2])
+    fresh_in.start()
     result_in.start()
-    for load in loads[:-1]:
-        load.start()
-    loads[-1].wait()
+    old.start()
+    tail[...] = pool_ref[kept:pool_dev]
+    fresh_in.wait()
     for d in range(n):
         @pl.when(plan_ref[d, cap + 1] < pool_dev)
         def _(d=d):
-            held[plan_ref[d, cap + 1]] = written_ref[d]
-    stores[-1].start()
+            tail[jnp.maximum(plan_ref[d, cap + 1] - kept, 0)] = fresh[d]
+    last.start()
     result_in.wait()
-    result_out.start()
-    for load, store in zip(loads[:-1], stores[:-1]):
-        load.wait()
-        store.start()
-    for store in stores:
-        store.wait()
-    result_out.wait()
+    result.start()
+    last.wait()
+    result.wait()
+    old.wait()
 
 
 def shards(queries, turn_cache, page_pool, prefix_tokens, prefix_table, write_table, assignment):
@@ -329,7 +320,7 @@
     tokens = max(cap, (n - 1) * wave) * page_size
     smem = pl.BlockSpec(memory_space=pltpu.SMEM)
     vmem = pl.BlockSpec(memory_space=pltpu.VMEM)
-    hbm = pl.BlockSpec(memory_space=pl.ANY)
+    hbm = pl.BlockSpec(memory_space=pltpu.HBM)
     bf16, f32 = jnp.bfloat16, jnp.float32
     plan = pl.pallas_call(
         functools.partial(plan_kernel, n, cap, pool_dev, page_size),
@@ -348,13 +339,12 @@
             jax.ShapeDtypeStruct(queries.shape, bf16),
             jax.ShapeDtypeStruct((n, page_rows, head_dim), bf16),
         ),
-        in_specs=[smem, hbm, hbm, hbm],
+        in_specs=[smem, hbm, hbm, vmem],
         out_specs=(vmem, vmem),
         scratch_shapes=[
             pltpu.VMEM(queries.shape, bf16),
             pltpu.VMEM((new_len // page_size, page_rows, head_dim), bf16),
-            pltpu.VMEM(pages.shape, bf16),
-            pltpu.SemaphoreType.DMA((3,)),
+            pltpu.SemaphoreType.DMA((2,)),
             pltpu.VMEM((n, cap * page_rows, head_dim), bf16),
             pltpu.VMEM((cap // wave, n - 1, wave * page_rows, head_dim), bf16),
             pltpu.VMEM((n - 1, max(cap % wave, 1) * page_rows, head_dim), bf16),
@@ -386,13 +376,13 @@
             jax.ShapeDtypeStruct(queries.shape, bf16),
             jax.ShapeDtypeStruct(pages.shape, bf16),
         ),
-        in_specs=[smem, vmem, hbm, hbm],
+        in_specs=[smem, hbm, hbm, vmem],
         out_specs=(hbm, hbm),
         scratch_shapes=[
-            pltpu.VMEM(pages.shape, bf16),
+            pltpu.VMEM((n, page_rows, head_dim), bf16),
             pltpu.VMEM(queries.shape, bf16),
-            pltpu.SemaphoreType.DMA((9,)),
-            pltpu.SemaphoreType.DMA((9,)),
+            pltpu.VMEM((n, page_rows, head_dim), bf16),
+            pltpu.SemaphoreType.DMA((3,)),
             pltpu.SemaphoreType.DMA((2,)),
         ],
         compiler_params=pltpu.CompilerParams(vmem_limit_bytes=56 * 1024 * 1024),

time: 128 us -> 128 us (level)
  no operation moved by 1% of the time
where the time goes in v2:
time: 128 us
  Pallas kernels  127 us (99%)
    pallas_call x1, Pallas kernels, shards(): pl.pallas_call(functools.partial(kernel, n, cap, wave, page_rows, row_blo...  120 us
    pallas_call x1, Pallas kernels, shards(): pl.pallas_call(functools.partial(merge_kernel, n, cap, pool_dev), out_sha...  5.77 us

profile of v2, /device:TPU:0, one launch (start us, length us, event | category | flops | bytes accessed | tf_op | source)
XLA Modules:
  0.0 127.6 jit_solution(18381631752677650058)
XLA Ops:
  0.6 1.6 %shard_map.86.plan_ref = s32[16,128]{1,0:T(8,128)} custom-call(s32[8]{0:T(128)} %assign_ref.1, s32[8]{0:T(128)} %tokens_ref.1, s32[8,128]{1,0:T(8,128)} %table_ref.1, s32[8,8]{1,0:T(8,128)} %write_ref.1), custom_call_target="tpu_custom_call" | custom-call | tf_op jit(solution)/shard_map/pallas_call | solution.py:325
  2.2 119.7 %shard_map.87 = (bf16[256,16,128]{2,1,0:T(8,128)(2,1)}, bf16[8,128,128]{2,1,0:T(8,128)(2,1)}) custom-call(s32[16,128]{1,0:T(8,128)} %shard_map.86.plan_ref, bf16[256,16,128]{2,1,0:T(8,128)(2,1)} %q_hbm.1, bf16[8,128,128]{2,1,0:T(8,128)(2,1)} %bitcast.5, bf16[160,128,128]{2,1,0:T(8,128)(2,1)} %bitcast.3), custom_call_target="tpu_custom_call" | custom-call | tf_op jit(solution)/shard_map/pallas_call | solution.py:336
  121.9 5.8 %shard_map.88 = (bf16[256,16,128]{2,1,0:T(8,128)(2,1)}, bf16[160,128,128]{2,1,0:T(8,128)(2,1)}) custom-call(s32[16,128]{1,0:T(8,128)} %shard_map.86.plan_ref, bf16[8,128,128]{2,1,0:T(8,128)(2,1)} %get-tuple-element.6.written_ref, bf16[256,16,128]{2,1,0:T(8,128)(2,1)} %get-tuple-element.7.attention_ref, bf16[160,128,128]{2,1,0:T(8,128)(2,1)} %bitcast.4), custom_call_target="tpu_custom_call" | custom-call | tf_op jit(solution)/shard_map/pallas_call | solution.py:373
